TPU v7x, 256 devices: a whole 4x4x8 slice. The times are simulated.
256 devices in a mesh: aux: 32 (over y, z), row: 8 (over x, core).
Axes of the slice: x: 4, y: 4, z: 8, core: 2. Of those that a mesh axis runs over, the one named last changes fastest.
Arguments:
- three_index: bfloat16 [256, 256, 128, 128], P('aux', 'row'), may hold values from -0.125 to 0.125
- coeffs: bfloat16 [16384, 256], P('aux'), may hold values from -0.375 to 0.375
- pair_owner: int32 [32, 256, 1], P('aux', 'row'), may hold values from 0 to 31; in each aligned block of 32 rows (0 to 31, 32 to 63, ..., all dimensions but the last counted through in order) at most 2 rows name the same one
- pair_tile: int32 [32, 256], P('aux', 'row'), may hold values from 0 to 3
- pair_mblock: int32 [32, 256], P('aux', 'row'), may hold values from 0 to 1
Outputs:
- exchange_matrix: float32 [2048, 2048], P('aux', 'row')
Inputs may be any that keep to these rules, and one draw needn't show every extreme that they name: `pair_owner`: among the 32 blocks of one device, no owner is named more than 2 times, and in every draw some device names some owner exactly 2 times; every owner is named somewhere.
All inputs are finite; a program needn't handle non-finite values.
Results may differ from a plain program's by a relative error of at most 0.00079.
Values may be sent and summed in bfloat16 or wider, within the bound.
A program may use at most 64 MiB of HBM per device.

v0:
```python
import jax
import jax.numpy as jnp
from jax import lax
from jax.sharding import PartitionSpec as P

ROWS_DEV = 256


def shards(three_index, coeffs, pair_owner, pair_tile, pair_mblock):
    aux_local, pair_count, block_size, _ = three_index.shape
    occupied = coeffs.shape[1]
    owned_blocks = coeffs.shape[0] // block_size
    row_blocks = ROWS_DEV // block_size
    owners = pair_owner.reshape(-1)
    tile_index = pair_tile.reshape(-1)
    mblocks = pair_mblock.reshape(-1)
    all_coeffs = lax.all_gather(coeffs, "aux", axis=0, tiled=True).reshape(-1, block_size, occupied)
    fetched = all_coeffs[owners * owned_blocks + tile_index]
    row_match = mblocks[None, :] == jnp.arange(row_blocks)[:, None]
    placed = jnp.where(row_match[:, :, None, None], fetched[None], jnp.zeros((), fetched.dtype))
    summed = jnp.einsum("pkml,bkli->pbmi", three_index, placed, preferred_element_type=jnp.float32)
    half_transform = summed.reshape(aux_local, ROWS_DEV, occupied).astype(jnp.bfloat16)
    partial_matrix = jnp.einsum(
        "pni,pmi->nm",
        lax.all_gather(half_transform, "row", axis=1, tiled=True),
        half_transform,
        preferred_element_type=jnp.float32,
    )
    exchange_matrix = lax.psum_scatter(partial_matrix, "aux", scatter_dimension=0, tiled=True)
    return exchange_matrix


def solution(mesh):
    placed = (
        P("aux", "row", None, None),
        P("aux", None),
        P("aux", "row", None),
        P("aux", "row"),
        P("aux", "row"),
    )
    return jax.shard_map(
        shards, mesh=mesh, in_specs=placed, out_specs=P("aux", "row"), check_vma=False
    )
```

profile of v0, /device:TPU:4, one launch (start us, length us, event | category | flops | bytes accessed | tf_op | source)
XLA Modules:
  0.0 403.8 jit_solution(15314207054277038996)
XLA Ops:
  6.5 0.0 all-gather.3.cloned.1.call-start
  6.5 0.7 all-gather.3.cloned.1.call-update
  7.3 0.0 all-gather.5.cloned.1.call-start
  7.3 0.7 fusion.16
  8.0 0.7 iota_compare_fusion
  8.7 102.8 %all-gather.3.cloned.1.call-done = bf16[16384,256]{1,0:T(8,128)(2,1)} async-done(((bf16[512,256]{1,0:T(8,128)(2,1)}), bf16[16384,256]{1,0:T(8,128)(2,1)}) %all-gather.3.cloned.1.call-update) | async-done | bytes 8388624 | tf_op jit(solution)/shard_map/all_gather | solution.py:17
  111.4 4.1 %gather_fusion = bf16[32,128,256]{2,1,0:T(8,128)(2,1)S(1)} fusion(bf16[128,128,256]{2,1,0:T(8,128)(2,1)} %bitcast.40, s32[1024]{0:T(1024)S(1)} %pad_clamp_fusion), kind=kCustom, calls=%fused_computation | custom fusion | bytes 4194432 | tf_op jit(solution)/shard_map/gather | solution.py:18
  115.5 7.1 %fusion.11 = bf16[8,2,128,256]{3,2,0,1:T(8,128)(2,1)S(1)} fusion(bf16[8,32,128,128]{3,2,1,0:T(8,128)(2,1)} %param.5, pred[2,32]{1,0:T(4,128)(4,1)S(1)} %iota_compare_fusion, bf16[32,128,256]{2,1,0:T(8,128)(2,1)S(1)} %gather_fusion), kind=kOutput, calls=%fused_computation.10 | convolution fusion | flops 4297588736 | bytes 11534400 | tf_op jit(solution)/shard_map/pkml,bkli->pbmi/dot_general | solution.py:21
  122.6 1.1 copy.6
  123.6 0.0 all-gather.5.cloned.1.call-update
  123.7 0.0 reduce-scatter.2.cloned.1.call-start
  123.7 48.4 %all-gather.5.cloned.1.call-done = bf16[8,2048,256]{2,1,0:T(8,128)(2,1)} async-done(((bf16[8,256,256]{2,1,0:T(8,128)(2,1)}), bf16[8,2048,256]{2,1,0:T(8,128)(2,1)}) %all-gather.5.cloned.1.call-update) | async-done | bytes 8388624 | tf_op jit(solution)/shard_map/all_gather | solution.py:25
  172.1 7.3 %convolution_bitcast_fusion = f32[2048,256]{1,0:T(8,128)} fusion(bf16[8,2048,256]{2,1,0:T(8,128)(2,1)} %all-gather.5.cloned.1.call-done, bf16[8,256,256]{2,1,0:T(8,128)(2,1)} %bitcast.39), kind=kOutput, calls=%fused_computation.6 | convolution fusion | flops 2147483648 | bytes 11534336 | tf_op jit(solution)/shard_map/pni,pmi->nm/dot_general | solution.py:23
  179.4 0.0 reduce-scatter.2.cloned.1.call-update
  179.4 217.8 %reduce-scatter.2.cloned.1.call-done = f32[64,256]{1,0:T(8,128)} async-done(((f32[2048,256]{1,0:T(8,128)}), f32[64,256]{1,0:T(8,128)}) %reduce-scatter.2.cloned.1.call-update) | async-done | bytes 65552 | tf_op jit(solution)/shard_map/reduce_scatter | solution.py:29
  (1 shorter events, 0.0 us)
Async XLA Ops:
  6.5 104.9 %all-gather.3.cloned.1.call-start = ((), (), s32[]{:S(2)}) async-start(), calls=%async_computation.1 | async-start | bytes 8650752 | tf_op jit(solution)/shard_map/all_gather | solution.py:17
  7.3 164.8 %all-gather.5.cloned.1.call-start = ((), (), s32[]{:S(2)}) async-start(), calls=%async_computation.2 | async-start | bytes 9437184 | tf_op jit(solution)/shard_map/all_gather | solution.py:25
  123.7 273.6 %reduce-scatter.2.cloned.1.call-start = ((), (), s32[]{:S(2)}) async-start(), calls=%async_computation.3 | async-start | bytes 2162688 | tf_op jit(solution)/shard_map/reduce_scatter | solution.py:29
Sparse Core Ops, SparseCore 0:
  9.9 101.4 all-gather.2
  123.8 48.2 all-gather.4
  179.5 217.6 reduce-scatter.1
where the time goes:
time: 404 us
  waiting for transfers between devices  370 us (92%)
  matrix products  14.4 us (4%)
  between operations  13.1 us (3%)
  local copies, waits for them, and re-layouts  5.13 us (1%)
    reduce_scatter x1, waiting for transfers between devices, shards(): lax.psum_scatter(partial_matrix, 'aux', scatter_dimension=0, tiled=True)  218 us
    all_gather x1, waiting for transfers between devices, shards(): lax.all_gather(coeffs, 'aux', axis=0, tiled=True)  103 us
    all_gather x1, waiting for transfers between devices, shards(): lax.all_gather(half_transform, 'row', axis=1, tiled=True)  48.4 us
  transfers between devices with their start and end apart: 3, of which 3 were waited for; matrix products, arithmetic and copies ran while one was open for 0% of the time, Pallas kernels for 0%

commit v1 on v0

v1 whole, which is shorter than its diff:
```python
import functools

import jax
import jax.numpy as jnp
from jax import lax
from jax.experimental import pallas as pl
from jax.experimental.pallas import tpu as pltpu
from jax.sharding import PartitionSpec as P

MESH = pl.DeviceIdType.MESH
NX, NY, NZ = 4, 4, 8
BLK = 128
F32, BF16 = jnp.float32, jnp.bfloat16


def broadcast_tree():
    parent = {}
    for dz in (1, 2, 3, 4):
        parent[0, dz] = (0, dz - 1)
    for dz in (-1, -2, -3):
        parent[0, dz] = (0, dz + 1)
    for dz in range(-3, 5):
        parent[1, dz] = (0, dz)
        parent[-1, dz] = (0, dz)
    parent[1, 4] = (1, 3)
    parent[2, 0] = (1, 0)
    for dz in (1, 2, 3):
        parent[2, dz] = (2, dz - 1)
    for dz in (-1, -2, -3, -4):
        parent[2, dz] = (2, dz + 1)
    return parent


PARENT = broadcast_tree()
ARRIVALS = [
    (1, 0), (-1, 0), (0, 1), (0, -1), (2, 0), (-1, 1), (0, 2), (0, -2), (1, 1), (-1, -1), (2, 1), (2, -1),
    (1, -1), (-1, 2), (0, 3), (0, -3), (1, 2), (-1, -2), (2, 2), (2, -2), (1, -2), (-1, 3), (0, 4), (1, 3),
    (2, -3), (-1, -3), (2, 3), (1, -3), (-1, 4), (1, 4), (2, -4),
]
SLOT = {offset: i for i, offset in enumerate(ARRIVALS)}


def height(offset):
    return 1 + max([height(o) for o in PARENT if PARENT[o] == offset], default=0)


CHILDREN = {
    offset: sorted([o for o in PARENT if PARENT[o] == offset], key=lambda o: -height(o))
    for offset in [(0, 0)] + ARRIVALS
}


def kernel(
    owner_ref, tile_ref, mblock_ref, coef_ref, t_hbm, out_ref,
    t_buf, c_buf0, c_buf1, rhs, acc, h_buf, g_buf, z_out, z_in, y_sum, y_in,
    t_sem, c_recv, c_send, cf_recv, cf_send, h_recv, h_send, hf_recv, hf_send, z_recv, z_send, y_recv, y_send,
):
    a, r = lax.axis_index("aux"), lax.axis_index("row")
    y, z = a // NZ, lax.rem(a, NZ)
    x, c = r // 2, lax.rem(r, 2)
    sign = 1 - 2 * c

    def at(dx=0, dy=0, dz=0, flip=0):
        return {
            "aux": lax.rem(y + dy + NY, NY) * NZ + lax.rem(z + dz + NZ, NZ),
            "row": lax.rem(x + dx + NX, NX) * 2 + lax.rem(c + flip, 2),
        }

    def copy(src, dst, send, recv, device):
        return pltpu.make_async_remote_copy(
            src_ref=src, dst_ref=dst, send_sem=send, recv_sem=recv, device_id=device, device_id_type=MESH
        )

    c_bufs = (c_buf0, c_buf1)
    sibling = at(flip=1)
    t_copy = pltpu.make_async_copy(t_hbm, t_buf, t_sem)
    t_copy.start()
    partners = [sibling]
    partners += [at(dx=e) for e in range(1, NX)]
    partners += [at(dy=e) for e in range(1, NY)]
    partners += [at(dz=e) for e in range(1, NZ)]
    barrier = pltpu.get_barrier_semaphore()
    for device in partners:
        pl.semaphore_signal(barrier, inc=1, device_id=device, device_id_type=MESH)
    for ch in range(2):
        for t in range(4):
            c_bufs[ch][a * 4 + t] = coef_ref[t * BLK:(t + 1) * BLK, ch * BLK:(ch + 1) * BLK]
    pl.semaphore_wait(barrier, len(partners))

    def relay(ch, offset):
        dy, dz = offset
        origin = lax.rem(y - sign * dy + NY, NY) * NZ + lax.rem(z - sign * dz + NZ, NZ)
        piece = c_bufs[ch].at[pl.ds(origin * 4 + 2 * c, 2)]
        if offset != (0, 0):
            copy(piece, piece, c_send.at[ch], c_recv.at[ch, SLOT[offset]], sibling).wait_recv()
        for child in CHILDREN[offset]:
            to = at(dy=sign * (child[0] - dy), dz=sign * (child[1] - dz))
            copy(piece, piece, c_send.at[ch], c_recv.at[ch, SLOT[child]], to).start()
        if offset != (0, 0):
            copy(piece, piece, cf_send.at[ch], cf_recv.at[ch], sibling).start()

    carried = c_buf0.at[pl.ds(0, 2 * len(ARRIVALS))]

    def wait_flipped(ch):
        copy(carried, carried, cf_send.at[ch], cf_recv.at[ch], sibling).wait_recv()

    def build_rhs(ch):
        for k in range(32):
            block = c_bufs[ch][owner_ref[k] * 4 + tile_ref[k]]
            zero = jnp.zeros_like(block)
            for b in range(2):
                rhs[k * BLK:(k + 1) * BLK, b * BLK:(b + 1) * BLK] = jnp.where(mblock_ref[k] == b, block, zero)

    def half_dot(g):
        lhs = jnp.concatenate([t_buf[:, 4 * g + j].reshape(8 * BLK, BLK) for j in range(4)], axis=1)
        product = jnp.dot(lhs, rhs[g * 512:(g + 1) * 512, :], preferred_element_type=F32)
        if g == 0:
            acc[...] = product
        else:
            acc[...] += product

    def store_half(ch):
        for p in range(8):
            for b in range(2):
                h_buf[ch, 0, c, b * BLK:(b + 1) * BLK, p * BLK:(p + 1) * BLK] = acc[
                    p * BLK:(p + 1) * BLK, b * BLK:(b + 1) * BLK
                ].astype(BF16)

    def send_half(ch, e):
        d = (NX - e) % NX
        return copy(h_buf.at[ch, 0, c], h_buf.at[ch, d, c], h_send.at[ch, e], h_recv.at[ch, d], at(dx=e))

    def flip_half(ch, d):
        ref = h_buf.at[ch, d, c]
        return copy(ref, ref, hf_send.at[ch, d], hf_recv.at[ch, d], sibling)

    def gram(d):
        for src in range(2):
            total = None
            for ch in range(2):
                part = lax.dot_general(
                    h_buf[ch, d, src], h_buf[ch, 0, c], (((1,), (1,)), ((), ())), preferred_element_type=F32
                )
                total = part if total is None else total + part
            g_buf[src * 256:(src + 1) * 256, :] = total
            z_out[d, src * 256:(src + 1) * 256, :] = total.astype(BF16)
        y_sum[d] = g_buf[pl.ds(pl.multiple_of(z * 64, 64), 64), :]

    def z_copy(d, e):
        rows = pl.ds(pl.multiple_of(lax.rem(z + e, NZ) * 64, 64), 64)
        return copy(z_out.at[d, rows], z_in.at[d, e - 1], z_send.at[d], z_recv.at[d], at(dz=e))

    def z_start(d):
        for e in (4, 3, 5, 2, 6, 1, 7):
            z_copy(d, e).start()

    def y_copy(d):
        plane = lax.rem(x + d, NX)
        slot = lax.rem(y - plane + 2 * NY - 1, NY)
        to = {"aux": plane * NZ + z, "row": r}
        return plane, copy(y_sum.at[d], y_in.at[slot], y_send.at[d], y_recv.at[slot], to)

    def z_finish(d):
        copy(z_in.at[d], z_in.at[d], z_send.at[d], z_recv.at[d], sibling).wait_recv()
        total = y_sum[d]
        for e in range(NZ - 1):
            total = total + z_in[d, e].astype(F32)
        y_sum[d] = total
        plane, send = y_copy(d)
        pl.when(plane != y)(send.start)

    relay(0, (0, 0))
    for i, offset in enumerate(ARRIVALS):
        relay(0, offset)
        if i == 15:
            relay(1, (0, 0))
    wait_flipped(0)
    t_copy.wait()
    build_rhs(0)
    later = list(ARRIVALS)
    for g in range(8):
        half_dot(g)
        relay(1, later.pop(0))
    store_half(0)
    flip_half(0, 0).start()
    send_half(0, 1).start()
    send_half(0, 3).start()
    for offset in later:
        relay(1, offset)
    wait_flipped(1)
    build_rhs(1)
    for g in range(8):
        half_dot(g)
    store_half(1)
    flip_half(1, 0).start()
    send_half(1, 1).start()
    send_half(1, 3).start()
    for d in (1, 3):
        flip = flip_half(0, d)
        send_half(0, NX - d).wait_recv()
        flip.start()
    flip_half(0, 0).wait_recv()
    flip_half(1, 0).wait_recv()
    gram(0)
    z_start(0)
    send_half(0, 2).start()
    send_half(1, 2).start()
    z_finish(0)
    for d in (1, 3):
        send_half(1, NX - d).wait_recv()
        flip_half(1, d).start()
    for d in (1, 3):
        flip_half(0, d).wait_recv()
        flip_half(1, d).wait_recv()
        gram(d)
        z_start(d)
    for d in (1, 3):
        z_finish(d)
    for ch in range(2):
        send_half(ch, 2).wait_recv()
        flip_half(ch, 2).start()
    for ch in range(2):
        flip_half(ch, 2).wait_recv()
    gram(2)
    z_start(2)
    z_finish(2)
    for slot in range(NY - 1):
        copy(y_in.at[slot], y_in.at[slot], y_send.at[0], y_recv.at[slot], sibling).wait_recv()
    out_ref[...] = y_sum[lax.rem(y - x + NY, NY)] + y_in[0] + y_in[1] + y_in[2]

    for ch in range(2):
        copy(carried, carried, c_send.at[ch], c_recv.at[ch, 0], sibling).wait_send()
        copy(carried, carried, cf_send.at[ch], cf_recv.at[ch], sibling).wait_send()
        for e in range(1, NX):
            send_half(ch, e).wait_send()
        for d in range(NX):
            flip_half(ch, d).wait_send()
    for d in range(NX):
        copy(z_in.at[d], z_in.at[d], z_send.at[d], z_recv.at[d], sibling).wait_send()
        plane, send = y_copy(d)
        pl.when(plane != y)(send.wait_send)


def shards(three_index, coeffs, pair_owner, pair_tile, pair_mblock):
    smem, vmem = pl.BlockSpec(memory_space=pltpu.SMEM), pl.BlockSpec(memory_space=pltpu.VMEM)
    dma = pltpu.SemaphoreType.DMA
    return pl.pallas_call(
        kernel,
        out_shape=jax.ShapeDtypeStruct((64, 256), F32),
        in_specs=[smem, smem, smem, vmem, pl.BlockSpec(memory_space=pl.ANY)],
        out_specs=vmem,
        scratch_shapes=[
            pltpu.VMEM((8, 32, BLK, BLK), BF16),
            pltpu.VMEM((128, BLK, BLK), BF16),
            pltpu.VMEM((128, BLK, BLK), BF16),
            pltpu.VMEM((32 * BLK, 256), BF16),
            pltpu.VMEM((8 * BLK, 256), F32),
            pltpu.VMEM((2, 4, 2, 256, 1024), BF16),
            pltpu.VMEM((512, 256), F32),
            pltpu.VMEM((4, 512, 256), BF16),
            pltpu.VMEM((4, 7, 64, 256), BF16),
            pltpu.VMEM((4, 64, 256), F32),
            pltpu.VMEM((4, 64, 256), F32),
            dma, dma((2, 31)), dma((2,)), dma((2,)), dma((2,)),
            dma((2, 4)), dma((2, 4)), dma((2, 4)), dma((2, 4)),
            dma((4,)), dma((4,)), dma((4,)), dma((4,)),
        ],
        compiler_params=pltpu.CompilerParams(
            collective_id=0, has_side_effects=True, vmem_limit_bytes=56 * 1024 * 1024
        ),
        name="exchange",
    )(pair_owner.reshape(32), pair_tile.reshape(32), pair_mblock.reshape(32), coeffs, three_index)


def solution(mesh):
    placed = (
        P("aux", "row", None, None),
        P("aux", None),
        P("aux", "row", None),
        P("aux", "row"),
        P("aux", "row"),
    )
    return jax.shard_map(
        shards, mesh=mesh, in_specs=placed, out_specs=P("aux", "row"), check_vma=False
    )
```

time: 404 us -> 122 us (0.30)
  waiting for transfers between devices: 370 us -> 0 us
  Pallas kernels: 0 us -> 120 us
  matrix products: 14.4 us -> 0 us
  between operations: 13.1 us -> 0.01 us
    reduce_scatter x1 -> x0, waiting for transfers between devices: 218 us -> none  [shards(): lax.psum_scatter(partial_matrix, 'aux', scatter_dimension=0, tiled=True)]
    all_gather x2 -> x0, waiting for transfers between devices: 151 us -> none  [the longest x1 103 us: shards(): lax.all_gather(coeffs, 'aux', axis=0, tiled=True)]
    pallas_call x0 -> x1, Pallas kernels: none -> 120 us  [shards(): pl.pallas_call(kernel, out_shape=jax.ShapeDtypeStruct((64, 256), F32), in...]
    dot_general x2 -> x0, matrix products: 14.4 us -> none  [the longest x1 7.35 us: shards(): jnp.einsum('pni,pmi->nm', lax.all_gather(half_transform, 'row', axis=1, t...]
    gather x1 -> x0, local copies, waits for them, and re-layouts: 4.06 us -> none  [shards(): fetched = all_coeffs[owners * owned_blocks + tile_index]]
  transfers between devices with their start and end apart: 3 -> 0, of which waited for: 3 -> 0; matrix products, arithmetic and copies ran while one was open for 0% -> 0% of each run, Pallas kernels for 0% -> 0%
where the time goes in v1:
time: 122 us
  Pallas kernels  120 us (98%)
  local copies, waits for them, and re-layouts  1.47 us (1%)
    pallas_call x1, Pallas kernels, shards(): pl.pallas_call(kernel, out_shape=jax.ShapeDtypeStruct((64, 256), F32), in...  120 us

profile of v1, /device:TPU:4, one launch (start us, length us, event | category | flops | bytes accessed | tf_op | source)
XLA Modules:
  0.0 121.7 jit_solution(3395242888165342452)
XLA Ops:
  0.0 120.2 %exchange.1 = f32[64,256]{1,0:T(8,128)} custom-call(s32[32]{0:T(128)} %bitcast.3, s32[32]{0:T(128)} %bitcast.4, s32[32]{0:T(128)} %bitcast.5, bf16[512,256]{1,0:T(8,128)(2,1)} %coef_ref.1, bf16[8,32,128,128]{3,2,1,0:T(8,128)(2,1)} %t_hbm.1), custom_call_target="tpu_custom_call" | custom-call | tf_op jit(solution)/shard_map/exchange/pallas_call | solution.py:247
  120.2 1.5 %copy.7 = f32[64,256]{1,0:T(8,128)} copy(f32[64,256]{1,0:T(8,128)} %exchange.1) | data formatting | bytes 131072

commit v2 on v1

--- a/solution.py
+++ b/solution.py
@@ -1,5 +1,3 @@
-import functools
-
 import jax
 import jax.numpy as jnp
 from jax import lax
@@ -13,52 +11,86 @@
 F32, BF16 = jnp.float32, jnp.bfloat16
 
 
-def broadcast_tree():
-    parent = {}
-    for dz in (1, 2, 3, 4):
-        parent[0, dz] = (0, dz - 1)
-    for dz in (-1, -2, -3):
-        parent[0, dz] = (0, dz + 1)
-    for dz in range(-3, 5):
-        parent[1, dz] = (0, dz)
-        parent[-1, dz] = (0, dz)
-    parent[1, 4] = (1, 3)
-    parent[2, 0] = (1, 0)
-    for dz in (1, 2, 3):
-        parent[2, dz] = (2, dz - 1)
-    for dz in (-1, -2, -3, -4):
-        parent[2, dz] = (2, dz + 1)
-    return parent
-
-
-PARENT = broadcast_tree()
-ARRIVALS = [
-    (1, 0), (-1, 0), (0, 1), (0, -1), (2, 0), (-1, 1), (0, 2), (0, -2), (1, 1), (-1, -1), (2, 1), (2, -1),
-    (1, -1), (-1, 2), (0, 3), (0, -3), (1, 2), (-1, -2), (2, 2), (2, -2), (1, -2), (-1, 3), (0, 4), (1, 3),
-    (2, -3), (-1, -3), (2, 3), (1, -3), (-1, 4), (1, 4), (2, -4),
-]
-SLOT = {offset: i for i, offset in enumerate(ARRIVALS)}
-
-
-def height(offset):
-    return 1 + max([height(o) for o in PARENT if PARENT[o] == offset], default=0)
-
-
-CHILDREN = {
-    offset: sorted([o for o in PARENT if PARENT[o] == offset], key=lambda o: -height(o))
-    for offset in [(0, 0)] + ARRIVALS
-}
+TREE = (
+    (0, 0, 0, ((0, 2, 0), (0, 6, 0), (1, 0, 0), (0, 7, 0),)),
+    (1, 0, 0, ((3, 0, 0),)),
+    (0, 1, 0, ((1, 1, 0), (2, 0, 0), (3, 0, 1),)),
+    (1, 3, 0, ((3, 7, 0), (3, 3, 0), (1, 0, 1), (2, 0, 0),)),
+    (0, 0, 2, ((3, 2, 0),)),
+    (0, 0, 6, ((0, 4, 0), (0, 5, 0), (1, 6, 0), (3, 6, 0),)),
+    (0, 0, 7, ((1, 7, 0),)),
+    (0, 1, 1, ((3, 1, -1), (0, 1, 0),)),
+    (0, 2, 0, ((2, 7, 0),)),
+    (0, 3, 0, ()),
+    (1, 3, 7, ((0, 7, 0), (1, 7, -1), (3, 5, 0), (2, 7, 0),)),
+    (1, 2, 0, ()),
+    (1, 1, 0, ((1, 1, 0),)),
+    (0, 3, 2, ((3, 3, 0), (1, 2, 1), (2, 2, 0),)),
+    (0, 1, 6, ((2, 6, 0),)),
+    (0, 3, 6, ((3, 5, 0),)),
+    (0, 1, 7, ((3, 7, 1),)),
+    (0, 3, 1, ((2, 1, 0),)),
+    (0, 0, 4, ((1, 4, 0), (0, 3, 0),)),
+    (0, 0, 1, ()),
+    (0, 0, 5, ((1, 5, 0), (2, 5, 0),)),
+    (1, 0, 7, ((0, 1, 0),)),
+    (1, 1, 7, ((1, 6, 0),)),
+    (1, 3, 3, ((1, 3, -1),)),
+    (1, 1, 1, ()),
+    (0, 1, 2, ()),
+    (1, 2, 7, ((2, 1, 0),)),
+    (0, 2, 7, ()),
+    (0, 2, 6, ()),
+    (0, 3, 3, ((1, 3, -1), (2, 3, 0),)),
+    (0, 3, 7, ()),
+    (0, 2, 2, ()),
+    (0, 1, 4, ((2, 4, 0), (3, 4, 1),)),
+    (0, 2, 1, ()),
+    (1, 1, 3, ((1, 2, 0), (1, 4, 0), (0, 3, 0), (2, 3, 0),)),
+    (0, 1, 5, ()),
+    (1, 3, 5, ((0, 5, 0), (2, 5, 0), (3, 4, 0),)),
+    (0, 3, 5, ()),
+    (1, 0, 1, ((0, 2, 0), (3, 1, 0),)),
+    (0, 1, 3, ()),
+    (0, 2, 5, ()),
+    (0, 3, 4, ()),
+    (0, 2, 3, ()),
+    (0, 0, 3, ()),
+    (0, 2, 4, ()),
+    (1, 0, 3, ()),
+    (1, 1, 6, ((2, 6, 0), (3, 6, -1),)),
+    (1, 2, 3, ()),
+    (1, 2, 1, ()),
+    (1, 1, 4, ((0, 4, 0), (1, 5, 0),)),
+    (1, 2, 5, ((2, 4, 0),)),
+    (1, 1, 2, ((2, 2, 0),)),
+    (1, 0, 5, ((0, 6, 0),)),
+    (1, 0, 2, ((3, 2, 0),)),
+    (1, 3, 1, ()),
+    (1, 3, 4, ()),
+    (1, 2, 6, ()),
+    (1, 3, 6, ()),
+    (1, 0, 4, ()),
+    (1, 1, 5, ()),
+    (1, 2, 4, ()),
+    (1, 2, 2, ()),
+    (1, 3, 2, ()),
+    (1, 0, 6, ()),
+)
+
+SLOT = {entry[:3]: i for i, entry in enumerate(TREE)}
 
 
 def kernel(
     owner_ref, tile_ref, mblock_ref, coef_ref, t_hbm, out_ref,
     t_buf, c_buf0, c_buf1, rhs, acc, h_buf, g_buf, z_out, z_in, y_sum, y_in,
-    t_sem, c_recv, c_send, cf_recv, cf_send, h_recv, h_send, hf_recv, hf_send, z_recv, z_send, y_recv, y_send,
+    t_sem, c_recv, c_send, cf_recv, cf_send, h_recv, h_send, f_recv, f_send, hf_recv, hf_send, z_recv, z_send, y_recv, y_send,
 ):
     a, r = lax.axis_index("aux"), lax.axis_index("row")
     y, z = a // NZ, lax.rem(a, NZ)
     x, c = r // 2, lax.rem(r, 2)
-    sign = 1 - 2 * c
+    sign_z = 1 - 2 * c
+    sign_y = sign_z * (1 - 2 * lax.rem(x, 2))
 
     def at(dx=0, dy=0, dz=0, flip=0):
         return {
@@ -76,7 +108,7 @@
     t_copy = pltpu.make_async_copy(t_hbm, t_buf, t_sem)
     t_copy.start()
     partners = [sibling]
-    partners += [at(dx=e) for e in range(1, NX)]
+    partners += [at(dx=e) for e in (1, 3)]
     partners += [at(dy=e) for e in range(1, NY)]
     partners += [at(dz=e) for e in range(1, NZ)]
     barrier = pltpu.get_barrier_semaphore()
@@ -87,19 +119,19 @@
             c_bufs[ch][a * 4 + t] = coef_ref[t * BLK:(t + 1) * BLK, ch * BLK:(ch + 1) * BLK]
     pl.semaphore_wait(barrier, len(partners))
 
-    def relay(ch, offset):
-        dy, dz = offset
-        origin = lax.rem(y - sign * dy + NY, NY) * NZ + lax.rem(z - sign * dz + NZ, NZ)
+    def relay(entry):
+        ch, dy, dz, children = entry
+        origin = lax.rem(y - sign_y * dy + NY, NY) * NZ + lax.rem(z - sign_z * dz + NZ, NZ)
         piece = c_bufs[ch].at[pl.ds(origin * 4 + 2 * c, 2)]
-        if offset != (0, 0):
-            copy(piece, piece, c_send.at[ch], c_recv.at[ch, SLOT[offset]], sibling).wait_recv()
-        for child in CHILDREN[offset]:
-            to = at(dy=sign * (child[0] - dy), dz=sign * (child[1] - dz))
-            copy(piece, piece, c_send.at[ch], c_recv.at[ch, SLOT[child]], to).start()
-        if offset != (0, 0):
+        if dy or dz:
+            copy(piece, piece, c_send.at[ch], c_recv.at[SLOT[ch, dy, dz]], sibling).wait_recv()
+        for child_dy, child_dz, dx in children:
+            to = at(dx=dx) if dx else at(dy=sign_y * (child_dy - dy), dz=sign_z * (child_dz - dz))
+            copy(piece, piece, c_send.at[ch], c_recv.at[SLOT[ch, child_dy, child_dz]], to).start()
+        if dy or dz:
             copy(piece, piece, cf_send.at[ch], cf_recv.at[ch], sibling).start()
 
-    carried = c_buf0.at[pl.ds(0, 2 * len(ARRIVALS))]
+    carried = c_buf0.at[pl.ds(0, 62)]
 
     def wait_flipped(ch):
         copy(carried, carried, cf_send.at[ch], cf_recv.at[ch], sibling).wait_recv()
@@ -129,6 +161,12 @@
     def send_half(ch, e):
         d = (NX - e) % NX
         return copy(h_buf.at[ch, 0, c], h_buf.at[ch, d, c], h_send.at[ch, e], h_recv.at[ch, d], at(dx=e))
+
+    def pass_half(ch, e):
+        d, rows = (NX - e) % NX, pl.ds(0 if e == 1 else BLK, BLK)
+        return copy(
+            h_buf.at[ch, d, c, rows], h_buf.at[ch, 2, c, rows], f_send.at[ch, e], f_recv.at[ch, e], at(dx=e)
+        )
 
     def flip_half(ch, d):
         ref = h_buf.at[ch, d, c]
@@ -169,46 +207,42 @@
         plane, send = y_copy(d)
         pl.when(plane != y)(send.start)
 
-    relay(0, (0, 0))
-    for i, offset in enumerate(ARRIVALS):
-        relay(0, offset)
-        if i == 15:
-            relay(1, (0, 0))
+    done = max(i for i, entry in enumerate(TREE) if entry[0] == 0) + 1
+    for entry in TREE[:done]:
+        relay(entry)
+    later = list(TREE[done:])
     wait_flipped(0)
     t_copy.wait()
     build_rhs(0)
-    later = list(ARRIVALS)
     for g in range(8):
         half_dot(g)
-        relay(1, later.pop(0))
+        if later:
+            relay(later.pop(0))
     store_half(0)
-    flip_half(0, 0).start()
     send_half(0, 1).start()
     send_half(0, 3).start()
-    for offset in later:
-        relay(1, offset)
+    flip_half(0, 0).start()
+    for entry in later:
+        relay(entry)
     wait_flipped(1)
     build_rhs(1)
     for g in range(8):
         half_dot(g)
     store_half(1)
-    flip_half(1, 0).start()
     send_half(1, 1).start()
     send_half(1, 3).start()
-    for d in (1, 3):
-        flip = flip_half(0, d)
-        send_half(0, NX - d).wait_recv()
-        flip.start()
-    flip_half(0, 0).wait_recv()
-    flip_half(1, 0).wait_recv()
-    gram(0)
-    z_start(0)
-    send_half(0, 2).start()
-    send_half(1, 2).start()
+    flip_half(1, 0).start()
+    for ch in range(2):
+        for d in (1, 3):
+            send_half(ch, NX - d).wait_recv()
+            pass_half(ch, NX - d).start()
+            flip_half(ch, d).start()
+        if ch == 0:
+            for src in range(2):
+                flip_half(src, 0).wait_recv()
+            gram(0)
+            z_start(0)
     z_finish(0)
-    for d in (1, 3):
-        send_half(1, NX - d).wait_recv()
-        flip_half(1, d).start()
     for d in (1, 3):
         flip_half(0, d).wait_recv()
         flip_half(1, d).wait_recv()
@@ -217,7 +251,8 @@
     for d in (1, 3):
         z_finish(d)
     for ch in range(2):
-        send_half(ch, 2).wait_recv()
+        for e in (1, 3):
+            pass_half(ch, e).wait_recv()
         flip_half(ch, 2).start()
     for ch in range(2):
         flip_half(ch, 2).wait_recv()
@@ -229,10 +264,11 @@
     out_ref[...] = y_sum[lax.rem(y - x + NY, NY)] + y_in[0] + y_in[1] + y_in[2]
 
     for ch in range(2):
-        copy(carried, carried, c_send.at[ch], c_recv.at[ch, 0], sibling).wait_send()
+        copy(carried, carried, c_send.at[ch], c_recv.at[0], sibling).wait_send()
         copy(carried, carried, cf_send.at[ch], cf_recv.at[ch], sibling).wait_send()
-        for e in range(1, NX):
+        for e in (1, 3):
             send_half(ch, e).wait_send()
+            pass_half(ch, e).wait_send()
         for d in range(NX):
             flip_half(ch, d).wait_send()
     for d in range(NX):
@@ -261,8 +297,8 @@
             pltpu.VMEM((4, 7, 64, 256), BF16),
             pltpu.VMEM((4, 64, 256), F32),
             pltpu.VMEM((4, 64, 256), F32),
-            dma, dma((2, 31)), dma((2,)), dma((2,)), dma((2,)),
-            dma((2, 4)), dma((2, 4)), dma((2, 4)), dma((2, 4)),
+            dma, dma((64,)), dma((2,)), dma((2,)), dma((2,)),
+            dma((2, 4)), dma((2, 4)), dma((2, 4)), dma((2, 4)), dma((2, 4)), dma((2, 4)),
             dma((4,)), dma((4,)), dma((4,)), dma((4,)),
         ],
         compiler_params=pltpu.CompilerParams(

time: 122 us -> 96.4 us (0.79)
  Pallas kernels: 120 us -> 94.6 us
    pallas_call x1, Pallas kernels: 120 us -> 94.6 us  [shards(): pl.pallas_call(kernel, out_shape=jax.ShapeDtypeStruct((64, 256), F32), in...]
where the time goes in v2:
time: 96.4 us; the launch traced here: 96.1 us
  Pallas kernels  94.6 us (98%)
  local copies, waits for them, and re-layouts  1.47 us (2%)
    pallas_call x1, Pallas kernels, shards(): pl.pallas_call(kernel, out_shape=jax.ShapeDtypeStruct((64, 256), F32), in...  94.6 us

profile of v2, /device:TPU:4, one launch (start us, length us, event | category | flops | bytes accessed | tf_op | source)
XLA Modules:
  0.0 96.1 jit_solution(2408772888285539618)
XLA Ops:
  0.0 94.6 %exchange.1 = f32[64,256]{1,0:T(8,128)} custom-call(s32[32]{0:T(128)} %bitcast.3, s32[32]{0:T(128)} %bitcast.4, s32[32]{0:T(128)} %bitcast.5, bf16[512,256]{1,0:T(8,128)(2,1)} %coef_ref.1, bf16[8,32,128,128]{3,2,1,0:T(8,128)(2,1)} %t_hbm.1), custom_call_target="tpu_custom_call" | custom-call | tf_op jit(solution)/shard_map/exchange/pallas_call | solution.py:283
  94.6 1.5 %copy.7 = f32[64,256]{1,0:T(8,128)} copy(f32[64,256]{1,0:T(8,128)} %exchange.1) | data formatting | bytes 131072

commit v3 on v2

--- a/solution.py
+++ b/solution.py
@@ -83,8 +83,9 @@
 
 def kernel(
     owner_ref, tile_ref, mblock_ref, coef_ref, t_hbm, out_ref,
-    t_buf, c_buf0, c_buf1, rhs, acc, h_buf, g_buf, z_out, z_in, y_sum, y_in,
-    t_sem, c_recv, c_send, cf_recv, cf_send, h_recv, h_send, f_recv, f_send, hf_recv, hf_send, z_recv, z_send, y_recv, y_send,
+    t_buf, c_buf0, c_buf1, rhs, acc, h_own, h_nbr, h_far, g_buf, z_out, z_in, y_sum, y_in, x_pad, x_out, x_in,
+    t_sem, c_recv, c_send, cf_recv, cf_send, n_recv, n_send, f_recv, f_send, of_recv, of_send, nf_recv, nf_send,
+    ff_recv, ff_send, z_recv, z_send, y_recv, y_send, x_recv, x_send,
 ):
     a, r = lax.axis_index("aux"), lax.axis_index("row")
     y, z = a // NZ, lax.rem(a, NZ)
@@ -111,13 +112,28 @@
     partners += [at(dx=e) for e in (1, 3)]
     partners += [at(dy=e) for e in range(1, NY)]
     partners += [at(dz=e) for e in range(1, NZ)]
+    mirrors = [{"aux": x * NZ + 4 * c + t, "row": y * 2 + z // 4} for t in range(4)]
     barrier = pltpu.get_barrier_semaphore()
     for device in partners:
         pl.semaphore_signal(barrier, inc=1, device_id=device, device_id_type=MESH)
+
+    @pl.when(x != y)
+    def _():
+        for device in mirrors:
+            pl.semaphore_signal(barrier, inc=1, device_id=device, device_id_type=MESH)
+
     for ch in range(2):
         for t in range(4):
             c_bufs[ch][a * 4 + t] = coef_ref[t * BLK:(t + 1) * BLK, ch * BLK:(ch + 1) * BLK]
-    pl.semaphore_wait(barrier, len(partners))
+
+    @pl.when(x == y)
+    def _():
+        pl.semaphore_wait(barrier, len(partners))
+
+    @pl.when(x != y)
+    def _():
+        pl.semaphore_wait(barrier, len(partners) + len(mirrors))
+
 
     def relay(entry):
         ch, dy, dz, children = entry
@@ -154,32 +170,49 @@
     def store_half(ch):
         for p in range(8):
             for b in range(2):
-                h_buf[ch, 0, c, b * BLK:(b + 1) * BLK, p * BLK:(p + 1) * BLK] = acc[
+                h_own[ch, c, p // 2, b * BLK:(b + 1) * BLK, p % 2 * BLK:(p % 2 + 1) * BLK] = acc[
                     p * BLK:(p + 1) * BLK, b * BLK:(b + 1) * BLK
                 ].astype(BF16)
 
-    def send_half(ch, e):
-        d = (NX - e) % NX
-        return copy(h_buf.at[ch, 0, c], h_buf.at[ch, d, c], h_send.at[ch, e], h_recv.at[ch, d], at(dx=e))
-
-    def pass_half(ch, e):
-        d, rows = (NX - e) % NX, pl.ds(0 if e == 1 else BLK, BLK)
+    def send_nbr(ch, side):
         return copy(
-            h_buf.at[ch, d, c, rows], h_buf.at[ch, 2, c, rows], f_send.at[ch, e], f_recv.at[ch, e], at(dx=e)
+            h_own.at[ch, c, pl.ds(2 * side, 2)], h_nbr.at[ch, side, c], n_send.at[ch, side], n_recv.at[ch, side],
+            at(dx=1 if side else 3),
         )
 
-    def flip_half(ch, d):
-        ref = h_buf.at[ch, d, c]
-        return copy(ref, ref, hf_send.at[ch, d], hf_recv.at[ch, d], sibling)
+    def send_far(ch, side):
+        to = lax.rem(x + (1 if side else 3), NX)
+        return copy(
+            h_nbr.at[ch, side, c, to // 2], h_far.at[ch, side, c], f_send.at[ch, side], f_recv.at[ch, side],
+            at(dx=1 if side else 3),
+        )
+
+    def flip_own(ch):
+        ref = h_own.at[ch, c]
+        return copy(ref, ref, of_send.at[ch], of_recv.at[ch], sibling)
+
+    def flip_nbr(ch, side):
+        ref = h_nbr.at[ch, side, c]
+        return copy(ref, ref, nf_send.at[ch, side], nf_recv.at[ch, side], sibling)
+
+    def flip_far(ch, side):
+        ref = h_far.at[ch, side, c]
+        return copy(ref, ref, ff_send.at[ch, side], ff_recv.at[ch, side], sibling)
 
     def gram(d):
         for src in range(2):
             total = None
             for ch in range(2):
-                part = lax.dot_general(
-                    h_buf[ch, d, src], h_buf[ch, 0, c], (((1,), (1,)), ((), ())), preferred_element_type=F32
-                )
-                total = part if total is None else total + part
+                if d == 0:
+                    terms = [(h_own[ch, src, q], h_own[ch, c, q]) for q in range(4)]
+                elif d == 2:
+                    terms = [(h_far[ch, j, src], h_own[ch, c, 2 * j + x // 2]) for j in range(2)]
+                else:
+                    side = d // 2
+                    terms = [(h_nbr[ch, side, src, j], h_own[ch, c, 2 * side + j]) for j in range(2)]
+                for rows, columns in terms:
+                    part = lax.dot_general(rows, columns, (((1,), (1,)), ((), ())), preferred_element_type=F32)
+                    total = part if total is None else total + part
             g_buf[src * 256:(src + 1) * 256, :] = total
             z_out[d, src * 256:(src + 1) * 256, :] = total.astype(BF16)
         y_sum[d] = g_buf[pl.ds(pl.multiple_of(z * 64, 64), 64), :]
@@ -219,9 +252,9 @@
         if later:
             relay(later.pop(0))
     store_half(0)
-    send_half(0, 1).start()
-    send_half(0, 3).start()
-    flip_half(0, 0).start()
+    for side in range(2):
+        send_nbr(0, side).start()
+    flip_own(0).start()
     for entry in later:
         relay(entry)
     wait_flipped(1)
@@ -229,48 +262,66 @@
     for g in range(8):
         half_dot(g)
     store_half(1)
-    send_half(1, 1).start()
-    send_half(1, 3).start()
-    flip_half(1, 0).start()
-    for ch in range(2):
-        for d in (1, 3):
-            send_half(ch, NX - d).wait_recv()
-            pass_half(ch, NX - d).start()
-            flip_half(ch, d).start()
+    for side in range(2):
+        send_nbr(1, side).start()
+    flip_own(1).start()
+    for ch in range(2):
+        for side in range(2):
+            send_nbr(ch, side).wait_recv()
+            send_far(ch, side).start()
+            flip_nbr(ch, side).start()
         if ch == 0:
-            for src in range(2):
-                flip_half(src, 0).wait_recv()
+            for own in range(2):
+                flip_own(own).wait_recv()
             gram(0)
             z_start(0)
+    for side in range(2):
+        for ch in range(2):
+            flip_nbr(ch, side).wait_recv()
+        gram(2 * side + 1)
+        z_start(2 * side + 1)
     z_finish(0)
-    for d in (1, 3):
-        flip_half(0, d).wait_recv()
-        flip_half(1, d).wait_recv()
-        gram(d)
-        z_start(d)
-    for d in (1, 3):
-        z_finish(d)
-    for ch in range(2):
-        for e in (1, 3):
-            pass_half(ch, e).wait_recv()
-        flip_half(ch, 2).start()
-    for ch in range(2):
-        flip_half(ch, 2).wait_recv()
+    for ch in range(2):
+        for side in range(2):
+            send_far(ch, side).wait_recv()
+            flip_far(ch, side).start()
+    for ch in range(2):
+        for side in range(2):
+            flip_far(ch, side).wait_recv()
     gram(2)
     z_start(2)
-    z_finish(2)
+    for d in (1, 3, 2):
+        z_finish(d)
     for slot in range(NY - 1):
         copy(y_in.at[slot], y_in.at[slot], y_send.at[0], y_recv.at[slot], sibling).wait_recv()
-    out_ref[...] = y_sum[lax.rem(y - x + NY, NY)] + y_in[0] + y_in[1] + y_in[2]
+    total = y_sum[lax.rem(y - x + NY, NY)] + y_in[0] + y_in[1] + y_in[2]
+
+    def mirror_copy(t):
+        return copy(x_out.at[pl.ds(t * 64, 64)], x_in.at[lax.rem(z, 4)], x_send, x_recv, mirrors[t])
+
+    out_ref[...] = total
+
+    @pl.when(x != y)
+    def _():
+        x_pad[...] = jnp.zeros_like(x_pad)
+        x_pad[pl.ds(pl.multiple_of(lax.rem(z, 2) * 64, 64), 64), :] = out_ref[...]
+        x_out[...] = x_pad[...].T
+        for t in range(4):
+            mirror_copy(t).start()
+        copy(x_in, x_in, x_send, x_recv, sibling).wait_recv()
+        out_ref[:, 0:BLK] += x_in[0] + x_in[1]
+        out_ref[:, BLK:2 * BLK] += x_in[2] + x_in[3]
+        copy(x_in, x_in, x_send, x_recv, sibling).wait_send()
 
     for ch in range(2):
         copy(carried, carried, c_send.at[ch], c_recv.at[0], sibling).wait_send()
         copy(carried, carried, cf_send.at[ch], cf_recv.at[ch], sibling).wait_send()
-        for e in (1, 3):
-            send_half(ch, e).wait_send()
-            pass_half(ch, e).wait_send()
-        for d in range(NX):
-            flip_half(ch, d).wait_send()
+        flip_own(ch).wait_send()
+        for side in range(2):
+            send_nbr(ch, side).wait_send()
+            send_far(ch, side).wait_send()
+            flip_nbr(ch, side).wait_send()
+            flip_far(ch, side).wait_send()
     for d in range(NX):
         copy(z_in.at[d], z_in.at[d], z_send.at[d], z_recv.at[d], sibling).wait_send()
         plane, send = y_copy(d)
@@ -291,15 +342,21 @@
             pltpu.VMEM((128, BLK, BLK), BF16),
             pltpu.VMEM((32 * BLK, 256), BF16),
             pltpu.VMEM((8 * BLK, 256), F32),
-            pltpu.VMEM((2, 4, 2, 256, 1024), BF16),
+            pltpu.VMEM((2, 2, 4, 256, 256), BF16),
+            pltpu.VMEM((2, 2, 2, 2, 256, 256), BF16),
+            pltpu.VMEM((2, 2, 2, 256, 256), BF16),
             pltpu.VMEM((512, 256), F32),
             pltpu.VMEM((4, 512, 256), BF16),
             pltpu.VMEM((4, 7, 64, 256), BF16),
             pltpu.VMEM((4, 64, 256), F32),
             pltpu.VMEM((4, 64, 256), F32),
+            pltpu.VMEM((BLK, 256), F32),
+            pltpu.VMEM((256, BLK), F32),
+            pltpu.VMEM((4, 64, BLK), F32),
             dma, dma((64,)), dma((2,)), dma((2,)), dma((2,)),
-            dma((2, 4)), dma((2, 4)), dma((2, 4)), dma((2, 4)), dma((2, 4)), dma((2, 4)),
-            dma((4,)), dma((4,)), dma((4,)), dma((4,)),
+            dma((2, 2)), dma((2, 2)), dma((2, 2)), dma((2, 2)), dma((2,)), dma((2,)),
+            dma((2, 2)), dma((2, 2)), dma((2, 2)), dma((2, 2)),
+            dma((4,)), dma((4,)), dma((4,)), dma((4,)), dma, dma,
         ],
         compiler_params=pltpu.CompilerParams(
             collective_id=0, has_side_effects=True, vmem_limit_bytes=56 * 1024 * 1024

time: 96.4 us -> 93 us (0.965)
  the two profiles are of different devices: /device:TPU:4 before, /device:TPU:17 now
where the time goes in v3:
time: 93 us; the launch traced here: 92.8 us
  Pallas kernels  91.4 us (98%)
  local copies, waits for them, and re-layouts  1.47 us (2%)
    pallas_call x1, Pallas kernels, shards(): pl.pallas_call(kernel, out_shape=jax.ShapeDtypeStruct((64, 256), F32), in...  91.4 us

profile of v3, /device:TPU:17, one launch (start us, length us, event | category | flops | bytes accessed | tf_op | source)
XLA Modules:
  0.0 92.8 jit_solution(12498545911587666623)
XLA Ops:
  0.0 91.4 %exchange.1 = f32[64,256]{1,0:T(8,128)} custom-call(s32[32]{0:T(128)} %bitcast.3, s32[32]{0:T(128)} %bitcast.4, s32[32]{0:T(128)} %bitcast.5, bf16[512,256]{1,0:T(8,128)(2,1)} %coef_ref.1, bf16[8,32,128,128]{3,2,1,0:T(8,128)(2,1)} %t_hbm.1), custom_call_target="tpu_custom_call" | custom-call | tf_op jit(solution)/shard_map/exchange/pallas_call | solution.py:334
  91.4 1.5 %copy.7 = f32[64,256]{1,0:T(8,128)} copy(f32[64,256]{1,0:T(8,128)} %exchange.1) | data formatting | bytes 131072

commit v4 on v3

--- a/solution.py
+++ b/solution.py
@@ -83,9 +83,11 @@
 
 def kernel(
     owner_ref, tile_ref, mblock_ref, coef_ref, t_hbm, out_ref,
-    t_buf, c_buf0, c_buf1, rhs, acc, h_own, h_nbr, h_far, g_buf, z_out, z_in, y_sum, y_in, x_pad, x_out, x_in,
+    t_buf, c_buf0, c_buf1, rhs, acc, h_own, h_nbr, h_far, g_buf, g_nbr, z_out, z_in, y_sum, y_in,
+    w_in, w_out, v_in, x_pad, x_out, x_in,
     t_sem, c_recv, c_send, cf_recv, cf_send, n_recv, n_send, f_recv, f_send, of_recv, of_send, nf_recv, nf_send,
-    ff_recv, ff_send, z_recv, z_send, y_recv, y_send, x_recv, x_send,
+    ff_recv, ff_send, z_recv, z_send, y_recv, y_send,
+    w_recv, w_send, v_recv, v_send, x_recv, x_send,
 ):
     a, r = lax.axis_index("aux"), lax.axis_index("row")
     y, z = a // NZ, lax.rem(a, NZ)
@@ -199,31 +201,78 @@
         ref = h_far.at[ch, side, c]
         return copy(ref, ref, ff_send.at[ch, side], ff_recv.at[ch, side], sibling)
 
-    def gram(d):
-        for src in range(2):
-            total = None
-            for ch in range(2):
-                if d == 0:
-                    terms = [(h_own[ch, src, q], h_own[ch, c, q]) for q in range(4)]
-                elif d == 2:
-                    terms = [(h_far[ch, j, src], h_own[ch, c, 2 * j + x // 2]) for j in range(2)]
-                else:
-                    side = d // 2
-                    terms = [(h_nbr[ch, side, src, j], h_own[ch, c, 2 * side + j]) for j in range(2)]
-                for rows, columns in terms:
-                    part = lax.dot_general(rows, columns, (((1,), (1,)), ((), ())), preferred_element_type=F32)
-                    total = part if total is None else total + part
-            g_buf[src * 256:(src + 1) * 256, :] = total
-            z_out[d, src * 256:(src + 1) * 256, :] = total.astype(BF16)
-        y_sum[d] = g_buf[pl.ds(pl.multiple_of(z * 64, 64), 64), :]
-
-    def z_copy(d, e):
+    def gram(d, src):
+        total = None
+        for ch in range(2):
+            if d == 0:
+                terms = [(h_own[ch, src, q], h_own[ch, c, q]) for q in range(4)]
+            elif d == 2:
+                terms = [(h_far[ch, j, src], h_own[ch, c, 2 * j + x // 2]) for j in range(2)]
+            else:
+                side = d // 2
+                terms = [(h_nbr[ch, side, src, j], h_own[ch, c, 2 * side + j]) for j in range(2)]
+            for rows, columns in terms:
+                part = lax.dot_general(rows, columns, (((1,), (1,)), ((), ())), preferred_element_type=F32)
+                total = part if total is None else total + part
+        rows = pl.ds(pl.multiple_of(src * 256, 256), 256)
+        if d % 2:
+            g_nbr[d // 2, rows, :] = total
+        else:
+            g_buf[rows, :] = total
+        z_out[d, rows, :] = total.astype(BF16)
+
+    cores = (c, lax.rem(c + 1, 2))
+    own_rows = pl.ds(pl.multiple_of(z * 64, 64), 64)
+
+    def z_start(d, src):
+        for t in range(4):
+            to = 4 * src + t
+            rows = pl.ds(pl.multiple_of(to * 64, 64), 64)
+            send = copy(
+                z_out.at[d, rows], z_in.at[d, lax.rem(to - z + 2 * NZ - 1, NZ)], z_send.at[d], z_recv.at[d],
+                {"aux": y * NZ + to, "row": r},
+            )
+            pl.when(to != z)(send.start)
+
+    def w_copy(d, rows):
+        plane = lax.rem(x + d, NX)
+        slot = lax.rem(y - plane + 2 * NY - 1, NY)
+        to = {"aux": plane * NZ + z, "row": r}
+        return plane, copy(z_out.at[d, rows], w_in.at[slot, rows], w_send.at[d // 2], w_recv.at[slot], to)
+
+    def w_start(d, src):
+        plane, send = w_copy(d, pl.ds(pl.multiple_of(src * 256, 256), 256))
+        pl.when(plane != y)(send.start)
+
+    def v_copy(e):
         rows = pl.ds(pl.multiple_of(lax.rem(z + e, NZ) * 64, 64), 64)
-        return copy(z_out.at[d, rows], z_in.at[d, e - 1], z_send.at[d], z_recv.at[d], at(dz=e))
-
-    def z_start(d):
+        return copy(w_out.at[rows], v_in.at[e - 1], v_send, v_recv, at(dz=e))
+
+    near = lax.rem(x + y, 2) == 1
+
+    def w_finish():
+        for slot in range(NY - 1):
+            copy(w_in.at[slot], w_in.at[slot], w_send.at[0], w_recv.at[slot], sibling).wait_recv()
+        total = g_nbr[lax.rem(y - x + NY, NY) // 2]
+        for slot in range(NY - 1):
+            total = total + w_in[slot].astype(F32)
+        w_out[...] = total.astype(BF16)
+        g_nbr[0] = total
         for e in (4, 3, 5, 2, 6, 1, 7):
-            z_copy(d, e).start()
+            v_copy(e).start()
+        y_sum[1] = g_nbr[0, own_rows, :]
+
+    def v_finish():
+        copy(v_in, v_in, v_send, v_recv, sibling).wait_recv()
+        total = y_sum[1]
+        for e in range(NZ - 1):
+            total = total + v_in[e].astype(F32)
+        out_ref[...] = total
+
+    def y_finish():
+        for slot in range(NY - 1):
+            copy(y_in.at[slot], y_in.at[slot], y_send.at[0], y_recv.at[slot], sibling).wait_recv()
+        out_ref[...] = y_sum[lax.rem(y - x + NY, NY)] + y_in[0] + y_in[1] + y_in[2]
 
     def y_copy(d):
         plane = lax.rem(x + d, NX)
@@ -268,38 +317,43 @@
     for ch in range(2):
         for side in range(2):
             send_nbr(ch, side).wait_recv()
+            flip_nbr(ch, side).start()
             send_far(ch, side).start()
-            flip_nbr(ch, side).start()
         if ch == 0:
             for own in range(2):
                 flip_own(own).wait_recv()
-            gram(0)
-            z_start(0)
+            for src in range(2):
+                gram(0, src)
+                z_start(0, src)
+            y_sum[0] = g_buf[own_rows, :]
+    for side in range(2):
+        gram(2 * side + 1, cores[0])
+        w_start(2 * side + 1, cores[0])
     for side in range(2):
         for ch in range(2):
             flip_nbr(ch, side).wait_recv()
-        gram(2 * side + 1)
-        z_start(2 * side + 1)
+        gram(2 * side + 1, cores[1])
+        w_start(2 * side + 1, cores[1])
     z_finish(0)
     for ch in range(2):
         for side in range(2):
             send_far(ch, side).wait_recv()
             flip_far(ch, side).start()
+    gram(2, cores[0])
+    z_start(2, cores[0])
     for ch in range(2):
         for side in range(2):
             flip_far(ch, side).wait_recv()
-    gram(2)
-    z_start(2)
-    for d in (1, 3, 2):
-        z_finish(d)
-    for slot in range(NY - 1):
-        copy(y_in.at[slot], y_in.at[slot], y_send.at[0], y_recv.at[slot], sibling).wait_recv()
-    total = y_sum[lax.rem(y - x + NY, NY)] + y_in[0] + y_in[1] + y_in[2]
+    gram(2, cores[1])
+    z_start(2, cores[1])
+    y_sum[2] = g_buf[own_rows, :]
+    pl.when(near)(w_finish)
+    z_finish(2)
+    pl.when(near)(v_finish)
+    pl.when(jnp.logical_not(near))(y_finish)
 
     def mirror_copy(t):
         return copy(x_out.at[pl.ds(t * 64, 64)], x_in.at[lax.rem(z, 4)], x_send, x_recv, mirrors[t])
-
-    out_ref[...] = total
 
     @pl.when(x != y)
     def _():
@@ -322,10 +376,14 @@
             send_far(ch, side).wait_send()
             flip_nbr(ch, side).wait_send()
             flip_far(ch, side).wait_send()
-    for d in range(NX):
+    for d in (0, 2):
         copy(z_in.at[d], z_in.at[d], z_send.at[d], z_recv.at[d], sibling).wait_send()
         plane, send = y_copy(d)
         pl.when(plane != y)(send.wait_send)
+    for d in (1, 3):
+        plane, send = w_copy(d, pl.ds(0, 512))
+        pl.when(plane != y)(send.wait_send)
+    pl.when(near)(copy(v_in, v_in, v_send, v_recv, sibling).wait_send)
 
 
 def shards(three_index, coeffs, pair_owner, pair_tile, pair_mblock):
@@ -346,17 +404,22 @@
             pltpu.VMEM((2, 2, 2, 2, 256, 256), BF16),
             pltpu.VMEM((2, 2, 2, 256, 256), BF16),
             pltpu.VMEM((512, 256), F32),
+            pltpu.VMEM((2, 512, 256), F32),
             pltpu.VMEM((4, 512, 256), BF16),
             pltpu.VMEM((4, 7, 64, 256), BF16),
             pltpu.VMEM((4, 64, 256), F32),
             pltpu.VMEM((4, 64, 256), F32),
+            pltpu.VMEM((4, 512, 256), BF16),
+            pltpu.VMEM((512, 256), BF16),
+            pltpu.VMEM((7, 64, 256), BF16),
             pltpu.VMEM((BLK, 256), F32),
             pltpu.VMEM((256, BLK), F32),
             pltpu.VMEM((4, 64, BLK), F32),
             dma, dma((64,)), dma((2,)), dma((2,)), dma((2,)),
             dma((2, 2)), dma((2, 2)), dma((2, 2)), dma((2, 2)), dma((2,)), dma((2,)),
             dma((2, 2)), dma((2, 2)), dma((2, 2)), dma((2, 2)),
-            dma((4,)), dma((4,)), dma((4,)), dma((4,)), dma, dma,
+            dma((4,)), dma((4,)), dma((4,)), dma((4,)),
+            dma((4,)), dma((2,)), dma, dma, dma, dma,
         ],
         compiler_params=pltpu.CompilerParams(
             collective_id=0, has_side_effects=True, vmem_limit_bytes=56 * 1024 * 1024

time: 93 us -> 87.2 us (0.938)
  the two profiles are of different devices: /device:TPU:17 before, /device:TPU:4 now
where the time goes in v4:
time: 87.2 us; the launch traced here: 86.3 us
  Pallas kernels  84.8 us (97%)
  local copies, waits for them, and re-layouts  1.47 us (2%)
    pallas_call x1, Pallas kernels, shards(): pl.pallas_call(kernel, out_shape=jax.ShapeDtypeStruct((64, 256), F32), in...  84.8 us

profile of v4, /device:TPU:4, one launch (start us, length us, event | category | flops | bytes accessed | tf_op | source)
XLA Modules:
  0.0 86.3 jit_solution(8324773913500221605)
XLA Ops:
  0.0 84.8 %exchange.1 = f32[64,256]{1,0:T(8,128)} custom-call(s32[32]{0:T(128)} %bitcast.3, s32[32]{0:T(128)} %bitcast.4, s32[32]{0:T(128)} %bitcast.5, bf16[512,256]{1,0:T(8,128)(2,1)} %coef_ref.1, bf16[8,32,128,128]{3,2,1,0:T(8,128)(2,1)} %t_hbm.1), custom_call_target="tpu_custom_call" | custom-call | tf_op jit(solution)/shard_map/exchange/pallas_call | solution.py:392
  84.8 1.5 %copy.7 = f32[64,256]{1,0:T(8,128)} copy(f32[64,256]{1,0:T(8,128)} %exchange.1) | data formatting | bytes 131072

commit v5 on v4

--- a/solution.py
+++ b/solution.py
@@ -298,8 +298,9 @@
     build_rhs(0)
     for g in range(8):
         half_dot(g)
-        if later:
-            relay(later.pop(0))
+        for _ in range(2):
+            if later:
+                relay(later.pop(0))
     store_half(0)
     for side in range(2):
         send_nbr(0, side).start()

time: 87.2 us -> 85.8 us (0.984)
  Pallas kernels: 84.8 us -> 83.1 us
    pallas_call x1, Pallas kernels: 84.8 us -> 83.1 us  [shards(): pl.pallas_call(kernel, out_shape=jax.ShapeDtypeStruct((64, 256), F32), in...]
where the time goes in v5:
time: 85.8 us; the launch traced here: 84.6 us
  Pallas kernels  83.1 us (97%)
  local copies, waits for them, and re-layouts  1.47 us (2%)
    pallas_call x1, Pallas kernels, shards(): pl.pallas_call(kernel, out_shape=jax.ShapeDtypeStruct((64, 256), F32), in...  83.1 us

profile of v5, /device:TPU:4, one launch (start us, length us, event | category | flops | bytes accessed | tf_op | source)
XLA Modules:
  0.0 84.6 jit_solution(230085155220003459)
XLA Ops:
  0.0 83.1 %exchange.1 = f32[64,256]{1,0:T(8,128)} custom-call(s32[32]{0:T(128)} %bitcast.3, s32[32]{0:T(128)} %bitcast.4, s32[32]{0:T(128)} %bitcast.5, bf16[512,256]{1,0:T(8,128)(2,1)} %coef_ref.1, bf16[8,32,128,128]{3,2,1,0:T(8,128)(2,1)} %t_hbm.1), custom_call_target="tpu_custom_call" | custom-call | tf_op jit(solution)/shard_map/exchange/pallas_call | solution.py:393
  83.1 1.5 %copy.7 = f32[64,256]{1,0:T(8,128)} copy(f32[64,256]{1,0:T(8,128)} %exchange.1) | data formatting | bytes 131072

commit v6 on v5

--- a/solution.py
+++ b/solution.py
@@ -281,7 +281,7 @@
         return plane, copy(y_sum.at[d], y_in.at[slot], y_send.at[d], y_recv.at[slot], to)
 
     def z_finish(d):
-        copy(z_in.at[d], z_in.at[d], z_send.at[d], z_recv.at[d], sibling).wait_recv()
+        copy(z_in.at[d, pl.ds(0, 7)], z_in.at[d, pl.ds(0, 7)], z_send.at[d], z_recv.at[d], sibling).wait_recv()
         total = y_sum[d]
         for e in range(NZ - 1):
             total = total + z_in[d, e].astype(F32)
@@ -378,7 +378,7 @@
             flip_nbr(ch, side).wait_send()
             flip_far(ch, side).wait_send()
     for d in (0, 2):
-        copy(z_in.at[d], z_in.at[d], z_send.at[d], z_recv.at[d], sibling).wait_send()
+        copy(z_in.at[d, pl.ds(0, 7)], z_in.at[d, pl.ds(0, 7)], z_send.at[d], z_recv.at[d], sibling).wait_send()
         plane, send = y_copy(d)
         pl.when(plane != y)(send.wait_send)
     for d in (1, 3):
@@ -407,7 +407,7 @@
             pltpu.VMEM((512, 256), F32),
             pltpu.VMEM((2, 512, 256), F32),
             pltpu.VMEM((4, 512, 256), BF16),
-            pltpu.VMEM((4, 7, 64, 256), BF16),
+            pltpu.VMEM((4, 8, 64, 256), BF16),
             pltpu.VMEM((4, 64, 256), F32),
             pltpu.VMEM((4, 64, 256), F32),
             pltpu.VMEM((4, 512, 256), BF16),

time: 85.8 us -> 85.8 us (level)
  no operation moved by 1% of the time
where the time goes in v6:
time: 85.8 us; the launch traced here: 84.6 us
  Pallas kernels  83.1 us (97%)
  local copies, waits for them, and re-layouts  1.47 us (2%)
    pallas_call x1, Pallas kernels, shards(): pl.pallas_call(kernel, out_shape=jax.ShapeDtypeStruct((64, 256), F32), in...  83.1 us

profile of v6, /device:TPU:4, one launch (start us, length us, event | category | flops | bytes accessed | tf_op | source)
XLA Modules:
  0.0 84.6 jit_solution(13846976729991785306)
XLA Ops:
  0.0 83.1 %exchange.1 = f32[64,256]{1,0:T(8,128)} custom-call(s32[32]{0:T(128)} %bitcast.3, s32[32]{0:T(128)} %bitcast.4, s32[32]{0:T(128)} %bitcast.5, bf16[512,256]{1,0:T(8,128)(2,1)} %coef_ref.1, bf16[8,32,128,128]{3,2,1,0:T(8,128)(2,1)} %t_hbm.1), custom_call_target="tpu_custom_call" | custom-call | tf_op jit(solution)/shard_map/exchange/pallas_call | solution.py:393
  83.1 1.5 %copy.7 = f32[64,256]{1,0:T(8,128)} copy(f32[64,256]{1,0:T(8,128)} %exchange.1) | data formatting | bytes 131072
